TPU v7x, 32 devices: a whole 2x2x4 slice. The times are simulated.
32 devices in a mesh: tm: 8 (over z, x), space: 4 (over y, core).
Axes of the slice: x: 2, y: 2, z: 4, core: 2. Of those that a mesh axis runs over, the one named last changes fastest.
Arguments:
- coarse_states: float32 [8, 6, 64, 512], P('tm', None, 'space'), may hold values from -6 to 6
- initial_condition: float32 [6, 64, 512], P(None, 'space'), may hold values from -6 to 6
- base_velocity: float32 [64, 512], P('space'), may hold values from 0.5 to 2
- base_shear: float32 [64, 512], P('space'), may hold values from -1 to 1
- base_stress: float32 [2, 64, 512], P(None, 'space'), may hold values from -1 to 1
- relax_rate: float32 [64, 512], P('space'), may hold values from 0.05 to 2
Outputs:
- corrected: float32 [8, 6, 64, 512], P('tm', None, 'space')
- residual: float32 [8, 6, 64, 512], P('tm', None, 'space')
All inputs are finite; a program needn't handle non-finite values.
Results may differ from a plain program's by a relative error of at most 0.00002.
Values sent between devices are 32-bit elements; how exact they have to be, the bound alone decides.
A program may use at most 64 MiB of HBM per device.

v0:
```python
import jax
import jax.numpy as jnp
from jax import lax
from jax.sharding import PartitionSpec as P

STEPS_SLAB = 8
CHAIN = 4


fine_step = 0.1
viscosity = 0.5
sound_sq = 1.0


def padded_2(cells, sides, width):
    for axis, dim in sides:
        count = lax.axis_size(axis)
        head = lax.slice_in_dim(cells, 0, width, axis=dim)
        tail = lax.slice_in_dim(cells, cells.shape[dim] - width, cells.shape[dim], axis=dim)
        cells = jnp.concatenate(
            [
                lax.ppermute(tail, axis, [(i, (i + 1) % count) for i in range(count)]),
                cells,
                lax.ppermute(head, axis, [((i + 1) % count, i) for i in range(count)]),
            ],
            axis=dim,
        )
    return cells


def passed_along(value, axis, steps):
    count = lax.axis_size(axis)
    initial, last = (max(0, -steps), min(count, count - steps))
    return lax.ppermute(value, axis, [(source, source + steps) for source in range(initial, last)])


def advance(extended, coef_rows, time_step):
    padded = jnp.pad(extended, ((0, 0), (0, 0), (1, 1)))
    center = padded[:, 1:-1, 1:-1]
    x_plus = padded[:, 2:, 1:-1]
    x_minus = padded[:, :-2, 1:-1]
    y_plus = padded[:, 1:-1, 2:]
    y_minus = padded[:, 1:-1, :-2]
    grad_x = 0.5 * (x_plus - x_minus)
    grad_y = 0.5 * (y_plus - y_minus)
    smooth = viscosity * (x_plus + x_minus + y_plus + y_minus - 4.0 * center)
    base_u = coef_rows[0]
    shear = coef_rows[1]
    stress_xx = coef_rows[2]
    stress_xy = coef_rows[3]
    rate = coef_rows[4]
    vel_v = center[1]
    str_a = center[3]
    str_b = center[4]
    str_c = center[5]
    tend_u = -base_u * grad_x[0] - shear * vel_v - grad_x[2] + grad_x[3] + grad_y[4] + smooth[0]
    tend_v = -base_u * grad_x[1] - grad_y[2] + grad_x[4] + grad_y[5] + smooth[1]
    tend_p = -sound_sq * (grad_x[0] + grad_y[1]) + smooth[2]
    tend_a = (
        -base_u * grad_x[3]
        + 2.0 * shear * str_b
        + 2.0 * (stress_xx * grad_x[0] + stress_xy * grad_y[0])
        + 2.0 * rate * grad_x[0]
        - rate * str_a
        + smooth[3]
    )
    tend_b = (
        -base_u * grad_x[4]
        + shear * str_c
        + stress_xy * grad_x[0]
        + stress_xx * grad_x[1]
        + stress_xy * grad_y[1]
        + rate * (grad_y[0] + grad_x[1])
        - rate * str_b
        + smooth[4]
    )
    tend_c = (
        -base_u * grad_x[5]
        + 2.0 * stress_xy * grad_x[1]
        + 2.0 * rate * grad_y[1]
        - rate * str_c
        + smooth[5]
    )
    tendency = jnp.stack([tend_u, tend_v, tend_p, tend_a, tend_b, tend_c], 0)
    return center + time_step * tendency


def one_step(field, coefficients, time_step):
    extended = padded_2(field, (("space", 1),), 1)
    return advance(extended, coefficients, time_step)


def per_device(
    coarse_states, initial_condition, base_velocity, base_shear, base_stress, relax_rate
):
    start_field = coarse_states[0]
    coefficients = jnp.concatenate(
        [base_velocity[None], base_shear[None], base_stress, relax_rate[None]], 0
    )
    slab_index = lax.axis_index("tm")
    coarse_dt = STEPS_SLAB * fine_step / 4.0

    def relaxed(field):
        for repeat in range(STEPS_SLAB - 1):
            field = one_step(field, coefficients, fine_step)
        return field

    first_end = one_step(relaxed(start_field), coefficients, fine_step)
    received = passed_along(first_end, "tm", 1)
    cpoint = jnp.where(slab_index == 0, start_field, received)
    second_end = one_step(relaxed(cpoint), coefficients, fine_step)
    earlier = passed_along(second_end, "tm", 1)
    residual = jnp.where(slab_index == 0, initial_condition - cpoint, earlier - cpoint)
    correction = residual
    for repeat in range(CHAIN - 1):
        moved = passed_along(correction, "tm", 1)
        coarse_field = moved
        for coarse_repeat in range(4):
            coarse_field = one_step(coarse_field, coefficients, coarse_dt)
        correction = residual + coarse_field
    corrected = cpoint + correction
    return (corrected[None], residual[None])


def solution(mesh):
    return jax.shard_map(
        per_device,
        mesh=mesh,
        in_specs=(
            P("tm", None, "space", None),
            P(None, "space", None),
            P("space", None),
            P("space", None),
            P(None, "space", None),
            P("space", None),
        ),
        out_specs=(P("tm", None, "space", None), P("tm", None, "space", None)),
        check_vma=False,
    )
```

profile of v0, /device:TPU:25, one launch (start us, length us, event | category | flops | bytes accessed | tf_op | source)
XLA Modules:
  0.0 197.5 jit_solution(17311115691919952533)
XLA Ops:
  4.3 2.3 %collective-permute-done = f32[6,1,512]{2,1,0:T(1,128)S(1)} collective-permute-done((f32[6,1,512]{2,1,0:T(1,128)S(1)}, f32[6,1,512]{2,1,0:T(1,128)S(1)}, u32[]{:S(2)}, u32[]{:S(2)}) %collective-permute-start) | collective-permute-done | bytes 12320 | tf_op jit(solution)/shard_map/ppermute | solution.py:24
  19.3 2.0 %collective-permute-done.4 = f32[6,1,512]{2,1,0:T(1,128)S(1)} collective-permute-done((f32[6,1,512]{2,1,0:T(1,128)S(1)}, f32[6,1,512]{2,1,0:T(1,128)S(1)}, u32[]{:S(2)}, u32[]{:S(2)}) %collective-permute-start.4) | collective-permute-done | bytes 12320 | tf_op jit(solution)/shard_map/ppermute | solution.py:24
  27.7 2.0 %collective-permute-done.6 = f32[6,1,512]{2,1,0:T(1,128)S(1)} collective-permute-done((f32[6,1,512]{2,1,0:T(1,128)S(1)}, f32[6,1,512]{2,1,0:T(1,128)S(1)}, u32[]{:S(2)}, u32[]{:S(2)}) %collective-permute-start.6) | collective-permute-done | bytes 12320 | tf_op jit(solution)/shard_map/ppermute | solution.py:24
  36.2 2.0 %collective-permute-done.8 = f32[6,1,512]{2,1,0:T(1,128)S(1)} collective-permute-done((f32[6,1,512]{2,1,0:T(1,128)S(1)}, f32[6,1,512]{2,1,0:T(1,128)S(1)}, u32[]{:S(2)}, u32[]{:S(2)}) %collective-permute-start.8) | collective-permute-done | bytes 12320 | tf_op jit(solution)/shard_map/ppermute | solution.py:24
  44.6 2.0 %collective-permute-done.10 = f32[6,1,512]{2,1,0:T(1,128)S(1)} collective-permute-done((f32[6,1,512]{2,1,0:T(1,128)S(1)}, f32[6,1,512]{2,1,0:T(1,128)S(1)}, u32[]{:S(2)}, u32[]{:S(2)}) %collective-permute-start.10) | collective-permute-done | bytes 12320 | tf_op jit(solution)/shard_map/ppermute | solution.py:24
  61.5 2.0 %collective-permute-done.14 = f32[6,1,512]{2,1,0:T(1,128)S(1)} collective-permute-done((f32[6,1,512]{2,1,0:T(1,128)S(1)}, f32[6,1,512]{2,1,0:T(1,128)S(1)}, u32[]{:S(2)}, u32[]{:S(2)}) %collective-permute-start.14) | collective-permute-done | bytes 12320 | tf_op jit(solution)/shard_map/ppermute | solution.py:24
  68.7 3.1 %collective-permute-start.16 = (f32[6,16,512]{2,1,0:T(8,128)S(1)}, f32[6,16,512]{2,1,0:T(8,128)S(1)}, u32[]{:S(2)}, u32[]{:S(2)}) collective-permute-start(f32[6,16,512]{2,1,0:T(8,128)S(1)} %multiply_add_fusion.17), channel_id=1, source_target_pairs={{0,4},{4,8},{8,12},{12,16},{16,20},{20,24},{24,28},{1,5},{5,9},{9,... | collective-permute-start | bytes 589832 | tf_op jit(solution)/shard_map/ppermute | solution.py:34
  71.8 5.7 %collective-permute-done.16 = f32[6,16,512]{2,1,0:T(8,128)S(1)} collective-permute-done((f32[6,16,512]{2,1,0:T(8,128)S(1)}, f32[6,16,512]{2,1,0:T(8,128)S(1)}, u32[]{:S(2)}, u32[]{:S(2)}) %collective-permute-start.16) | collective-permute-done | bytes 196640 | tf_op jit(solution)/shard_map/ppermute | solution.py:34
  79.8 2.3 %collective-permute-done.17 = f32[6,1,512]{2,1,0:T(1,128)S(1)} collective-permute-done((f32[6,1,512]{2,1,0:T(1,128)S(1)}, f32[6,1,512]{2,1,0:T(1,128)S(1)}, u32[]{:S(2)}, u32[]{:S(2)}) %collective-permute-start.17) | collective-permute-done | bytes 12320 | tf_op jit(solution)/shard_map/ppermute | solution.py:24
  84.0 2.0 %collective-permute-done.19 = f32[6,1,512]{2,1,0:T(1,128)S(1)} collective-permute-done((f32[6,1,512]{2,1,0:T(1,128)S(1)}, f32[6,1,512]{2,1,0:T(1,128)S(1)}, u32[]{:S(2)}, u32[]{:S(2)}) %collective-permute-start.19) | collective-permute-done | bytes 12320 | tf_op jit(solution)/shard_map/ppermute | solution.py:24
  87.9 2.0 %collective-permute-done.21 = f32[6,1,512]{2,1,0:T(1,128)S(1)} collective-permute-done((f32[6,1,512]{2,1,0:T(1,128)S(1)}, f32[6,1,512]{2,1,0:T(1,128)S(1)}, u32[]{:S(2)}, u32[]{:S(2)}) %collective-permute-start.21) | collective-permute-done | bytes 12320 | tf_op jit(solution)/shard_map/ppermute | solution.py:24
  91.8 2.0 %collective-permute-done.23 = f32[6,1,512]{2,1,0:T(1,128)S(1)} collective-permute-done((f32[6,1,512]{2,1,0:T(1,128)S(1)}, f32[6,1,512]{2,1,0:T(1,128)S(1)}, u32[]{:S(2)}, u32[]{:S(2)}) %collective-permute-start.23) | collective-permute-done | bytes 12320 | tf_op jit(solution)/shard_map/ppermute | solution.py:24
  95.7 2.0 %collective-permute-done.25 = f32[6,1,512]{2,1,0:T(1,128)S(1)} collective-permute-done((f32[6,1,512]{2,1,0:T(1,128)S(1)}, f32[6,1,512]{2,1,0:T(1,128)S(1)}, u32[]{:S(2)}, u32[]{:S(2)}) %collective-permute-start.25) | collective-permute-done | bytes 12320 | tf_op jit(solution)/shard_map/ppermute | solution.py:24
  99.5 2.0 %collective-permute-done.27 = f32[6,1,512]{2,1,0:T(1,128)S(1)} collective-permute-done((f32[6,1,512]{2,1,0:T(1,128)S(1)}, f32[6,1,512]{2,1,0:T(1,128)S(1)}, u32[]{:S(2)}, u32[]{:S(2)}) %collective-permute-start.27) | collective-permute-done | bytes 12320 | tf_op jit(solution)/shard_map/ppermute | solution.py:24
  103.4 2.2 %collective-permute-done.29 = f32[6,1,512]{2,1,0:T(1,128)S(1)} collective-permute-done((f32[6,1,512]{2,1,0:T(1,128)S(1)}, f32[6,1,512]{2,1,0:T(1,128)S(1)}, u32[]{:S(2)}, u32[]{:S(2)}) %collective-permute-start.29) | collective-permute-done | bytes 12320 | tf_op jit(solution)/shard_map/ppermute | solution.py:24
  107.5 2.0 %collective-permute-done.31 = f32[6,1,512]{2,1,0:T(1,128)S(1)} collective-permute-done((f32[6,1,512]{2,1,0:T(1,128)S(1)}, f32[6,1,512]{2,1,0:T(1,128)S(1)}, u32[]{:S(2)}, u32[]{:S(2)}) %collective-permute-start.31) | collective-permute-done | bytes 12320 | tf_op jit(solution)/shard_map/ppermute | solution.py:24
  110.1 2.4 %collective-permute-start.33 = (f32[6,16,512]{2,1,0:T(8,128)S(1)}, f32[6,16,512]{2,1,0:T(8,128)S(1)}, u32[]{:S(2)}, u32[]{:S(2)}) collective-permute-start(f32[6,16,512]{2,1,0:T(8,128)S(1)} %multiply_add_fusion.9), channel_id=1, source_target_pairs={{0,4},{4,8},{8,12},{12,16},{16,20},{20,24},{24,28},{1,5},{5,9},{9,... | collective-permute-start | bytes 589832 | tf_op jit(solution)/shard_map/ppermute | solution.py:34
  112.5 6.4 %collective-permute-done.33 = f32[6,16,512]{2,1,0:T(8,128)S(1)} collective-permute-done((f32[6,16,512]{2,1,0:T(8,128)S(1)}, f32[6,16,512]{2,1,0:T(8,128)S(1)}, u32[]{:S(2)}, u32[]{:S(2)}) %collective-permute-start.33) | collective-permute-done | bytes 196640 | tf_op jit(solution)/shard_map/ppermute | solution.py:34
  120.8 7.5 %collective-permute-done.34 = f32[6,16,512]{2,1,0:T(8,128)S(1)} collective-permute-done((f32[6,16,512]{2,1,0:T(8,128)S(1)}, f32[6,16,512]{2,1,0:T(8,128)S(1)}, u32[]{:S(2)}, u32[]{:S(2)}) %collective-permute-start.34) | collective-permute-done | bytes 196640 | tf_op jit(solution)/shard_map/ppermute | solution.py:34
  130.5 2.3 %collective-permute-done.35 = f32[6,1,512]{2,1,0:T(1,128)S(1)} collective-permute-done((f32[6,1,512]{2,1,0:T(1,128)S(1)}, f32[6,1,512]{2,1,0:T(1,128)S(1)}, u32[]{:S(2)}, u32[]{:S(2)}) %collective-permute-start.35) | collective-permute-done | bytes 12320 | tf_op jit(solution)/shard_map/ppermute | solution.py:24
  134.7 2.0 %collective-permute-done.37 = f32[6,1,512]{2,1,0:T(1,128)S(1)} collective-permute-done((f32[6,1,512]{2,1,0:T(1,128)S(1)}, f32[6,1,512]{2,1,0:T(1,128)S(1)}, u32[]{:S(2)}, u32[]{:S(2)}) %collective-permute-start.37) | collective-permute-done | bytes 12320 | tf_op jit(solution)/shard_map/ppermute | solution.py:24
  138.6 2.0 %collective-permute-done.39 = f32[6,1,512]{2,1,0:T(1,128)S(1)} collective-permute-done((f32[6,1,512]{2,1,0:T(1,128)S(1)}, f32[6,1,512]{2,1,0:T(1,128)S(1)}, u32[]{:S(2)}, u32[]{:S(2)}) %collective-permute-start.39) | collective-permute-done | bytes 12320 | tf_op jit(solution)/shard_map/ppermute | solution.py:24
  142.4 2.0 %collective-permute-done.41 = f32[6,1,512]{2,1,0:T(1,128)S(1)} collective-permute-done((f32[6,1,512]{2,1,0:T(1,128)S(1)}, f32[6,1,512]{2,1,0:T(1,128)S(1)}, u32[]{:S(2)}, u32[]{:S(2)}) %collective-permute-start.41) | collective-permute-done | bytes 12320 | tf_op jit(solution)/shard_map/ppermute | solution.py:24
  147.0 7.6 %collective-permute-done.43 = f32[6,16,512]{2,1,0:T(8,128)S(1)} collective-permute-done((f32[6,16,512]{2,1,0:T(8,128)S(1)}, f32[6,16,512]{2,1,0:T(8,128)S(1)}, u32[]{:S(2)}, u32[]{:S(2)}) %collective-permute-start.43) | collective-permute-done | bytes 196640 | tf_op jit(solution)/shard_map/ppermute | solution.py:34
  156.4 2.3 %collective-permute-done.44 = f32[6,1,512]{2,1,0:T(1,128)S(1)} collective-permute-done((f32[6,1,512]{2,1,0:T(1,128)S(1)}, f32[6,1,512]{2,1,0:T(1,128)S(1)}, u32[]{:S(2)}, u32[]{:S(2)}) %collective-permute-start.44) | collective-permute-done | bytes 12320 | tf_op jit(solution)/shard_map/ppermute | solution.py:24
  160.6 2.0 %collective-permute-done.46 = f32[6,1,512]{2,1,0:T(1,128)S(1)} collective-permute-done((f32[6,1,512]{2,1,0:T(1,128)S(1)}, f32[6,1,512]{2,1,0:T(1,128)S(1)}, u32[]{:S(2)}, u32[]{:S(2)}) %collective-permute-start.46) | collective-permute-done | bytes 12320 | tf_op jit(solution)/shard_map/ppermute | solution.py:24
  164.5 2.0 %collective-permute-done.48 = f32[6,1,512]{2,1,0:T(1,128)S(1)} collective-permute-done((f32[6,1,512]{2,1,0:T(1,128)S(1)}, f32[6,1,512]{2,1,0:T(1,128)S(1)}, u32[]{:S(2)}, u32[]{:S(2)}) %collective-permute-start.48) | collective-permute-done | bytes 12320 | tf_op jit(solution)/shard_map/ppermute | solution.py:24
  168.3 2.0 %collective-permute-done.50 = f32[6,1,512]{2,1,0:T(1,128)S(1)} collective-permute-done((f32[6,1,512]{2,1,0:T(1,128)S(1)}, f32[6,1,512]{2,1,0:T(1,128)S(1)}, u32[]{:S(2)}, u32[]{:S(2)}) %collective-permute-start.50) | collective-permute-done | bytes 12320 | tf_op jit(solution)/shard_map/ppermute | solution.py:24
  172.9 7.8 %collective-permute-done.52 = f32[6,16,512]{2,1,0:T(8,128)S(1)} collective-permute-done((f32[6,16,512]{2,1,0:T(8,128)S(1)}, f32[6,16,512]{2,1,0:T(8,128)S(1)}, u32[]{:S(2)}, u32[]{:S(2)}) %collective-permute-start.52) | collective-permute-done | bytes 196640 | tf_op jit(solution)/shard_map/ppermute | solution.py:34
  182.2 2.3 %collective-permute-done.53 = f32[6,1,512]{2,1,0:T(1,128)S(1)} collective-permute-done((f32[6,1,512]{2,1,0:T(1,128)S(1)}, f32[6,1,512]{2,1,0:T(1,128)S(1)}, u32[]{:S(2)}, u32[]{:S(2)}) %collective-permute-start.53) | collective-permute-done | bytes 12320 | tf_op jit(solution)/shard_map/ppermute | solution.py:24
  186.4 2.0 %collective-permute-done.55 = f32[6,1,512]{2,1,0:T(1,128)S(1)} collective-permute-done((f32[6,1,512]{2,1,0:T(1,128)S(1)}, f32[6,1,512]{2,1,0:T(1,128)S(1)}, u32[]{:S(2)}, u32[]{:S(2)}) %collective-permute-start.55) | collective-permute-done | bytes 12320 | tf_op jit(solution)/shard_map/ppermute | solution.py:24
  190.3 2.0 %collective-permute-done.57 = f32[6,1,512]{2,1,0:T(1,128)S(1)} collective-permute-done((f32[6,1,512]{2,1,0:T(1,128)S(1)}, f32[6,1,512]{2,1,0:T(1,128)S(1)}, u32[]{:S(2)}, u32[]{:S(2)}) %collective-permute-start.57) | collective-permute-done | bytes 12320 | tf_op jit(solution)/shard_map/ppermute | solution.py:24
  (386 shorter events, 103.2 us)
Async XLA Ops:
  3.5 3.1 %collective-permute-start = (f32[6,1,512]{2,1,0:T(1,128)S(1)}, f32[6,1,512]{2,1,0:T(1,128)S(1)}, u32[]{:S(2)}, u32[]{:S(2)}) collective-permute-start(f32[6,1,512]{2,1,0:T(1,128)S(1)} %get-tuple-element.141), channel_id=1, source_target_pairs={{1,0},{2,1},{3,2},{0,3},{5,4},{6,5},{7,6},{4,7},{9,8},{10,9},{11,1... | collective-permute-start | bytes 36872 | tf_op jit(solution)/shard_map/ppermute | solution.py:24
  9.7 3.2 %collective-permute-start.2 = (f32[6,1,512]{2,1,0:T(1,128)S(1)}, f32[6,1,512]{2,1,0:T(1,128)S(1)}, u32[]{:S(2)}, u32[]{:S(2)}) collective-permute-start(f32[6,1,512]{2,1,0:T(1,128)S(1)} %get-tuple-element.139), channel_id=1, source_target_pairs={{1,0},{2,1},{3,2},{0,3},{5,4},{6,5},{7,6},{4,7},{9,8},{10,9},{11,1... | collective-permute-start | bytes 36872 | tf_op jit(solution)/shard_map/ppermute | solution.py:24
  18.1 3.2 %collective-permute-start.4 = (f32[6,1,512]{2,1,0:T(1,128)S(1)}, f32[6,1,512]{2,1,0:T(1,128)S(1)}, u32[]{:S(2)}, u32[]{:S(2)}) collective-permute-start(f32[6,1,512]{2,1,0:T(1,128)S(1)} %get-tuple-element.137), channel_id=1, source_target_pairs={{1,0},{2,1},{3,2},{0,3},{5,4},{6,5},{7,6},{4,7},{9,8},{10,9},{11,1... | collective-permute-start | bytes 36872 | tf_op jit(solution)/shard_map/ppermute | solution.py:24
  26.6 3.2 %collective-permute-start.6 = (f32[6,1,512]{2,1,0:T(1,128)S(1)}, f32[6,1,512]{2,1,0:T(1,128)S(1)}, u32[]{:S(2)}, u32[]{:S(2)}) collective-permute-start(f32[6,1,512]{2,1,0:T(1,128)S(1)} %get-tuple-element.135), channel_id=1, source_target_pairs={{1,0},{2,1},{3,2},{0,3},{5,4},{6,5},{7,6},{4,7},{9,8},{10,9},{11,1... | collective-permute-start | bytes 36872 | tf_op jit(solution)/shard_map/ppermute | solution.py:24
  35.0 3.2 %collective-permute-start.8 = (f32[6,1,512]{2,1,0:T(1,128)S(1)}, f32[6,1,512]{2,1,0:T(1,128)S(1)}, u32[]{:S(2)}, u32[]{:S(2)}) collective-permute-start(f32[6,1,512]{2,1,0:T(1,128)S(1)} %get-tuple-element.133), channel_id=1, source_target_pairs={{1,0},{2,1},{3,2},{0,3},{5,4},{6,5},{7,6},{4,7},{9,8},{10,9},{11,1... | collective-permute-start | bytes 36872 | tf_op jit(solution)/shard_map/ppermute | solution.py:24
  43.5 3.2 %collective-permute-start.10 = (f32[6,1,512]{2,1,0:T(1,128)S(1)}, f32[6,1,512]{2,1,0:T(1,128)S(1)}, u32[]{:S(2)}, u32[]{:S(2)}) collective-permute-start(f32[6,1,512]{2,1,0:T(1,128)S(1)} %get-tuple-element.131), channel_id=1, source_target_pairs={{1,0},{2,1},{3,2},{0,3},{5,4},{6,5},{7,6},{4,7},{9,8},{10,9},{11,1... | collective-permute-start | bytes 36872 | tf_op jit(solution)/shard_map/ppermute | solution.py:24
  51.9 3.2 %collective-permute-start.12 = (f32[6,1,512]{2,1,0:T(1,128)S(1)}, f32[6,1,512]{2,1,0:T(1,128)S(1)}, u32[]{:S(2)}, u32[]{:S(2)}) collective-permute-start(f32[6,1,512]{2,1,0:T(1,128)S(1)} %get-tuple-element.129), channel_id=1, source_target_pairs={{1,0},{2,1},{3,2},{0,3},{5,4},{6,5},{7,6},{4,7},{9,8},{10,9},{11,1... | collective-permute-start | bytes 36872 | tf_op jit(solution)/shard_map/ppermute | solution.py:24
  60.3 3.2 %collective-permute-start.14 = (f32[6,1,512]{2,1,0:T(1,128)S(1)}, f32[6,1,512]{2,1,0:T(1,128)S(1)}, u32[]{:S(2)}, u32[]{:S(2)}) collective-permute-start(f32[6,1,512]{2,1,0:T(1,128)S(1)} %get-tuple-element.127), channel_id=1, source_target_pairs={{1,0},{2,1},{3,2},{0,3},{5,4},{6,5},{7,6},{4,7},{9,8},{10,9},{11,1... | collective-permute-start | bytes 36872 | tf_op jit(solution)/shard_map/ppermute | solution.py:24
  68.7 8.8 %collective-permute-start.16 = (f32[6,16,512]{2,1,0:T(8,128)S(1)}, f32[6,16,512]{2,1,0:T(8,128)S(1)}, u32[]{:S(2)}, u32[]{:S(2)}) collective-permute-start(f32[6,16,512]{2,1,0:T(8,128)S(1)} %multiply_add_fusion.17), channel_id=1, source_target_pairs={{0,4},{4,8},{8,12},{12,16},{16,20},{20,24},{24,28},{1,5},{5,9},{9,... | collective-permute-start | bytes 589832 | tf_op jit(solution)/shard_map/ppermute | solution.py:34
  79.0 3.1 %collective-permute-start.17 = (f32[6,1,512]{2,1,0:T(1,128)S(1)}, f32[6,1,512]{2,1,0:T(1,128)S(1)}, u32[]{:S(2)}, u32[]{:S(2)}) collective-permute-start(f32[6,1,512]{2,1,0:T(1,128)S(1)} %get-tuple-element.125), channel_id=1, source_target_pairs={{1,0},{2,1},{3,2},{0,3},{5,4},{6,5},{7,6},{4,7},{9,8},{10,9},{11,1... | collective-permute-start | bytes 36872 | tf_op jit(solution)/shard_map/ppermute | solution.py:24
  82.9 3.2 %collective-permute-start.19 = (f32[6,1,512]{2,1,0:T(1,128)S(1)}, f32[6,1,512]{2,1,0:T(1,128)S(1)}, u32[]{:S(2)}, u32[]{:S(2)}) collective-permute-start(f32[6,1,512]{2,1,0:T(1,128)S(1)} %get-tuple-element.123), channel_id=1, source_target_pairs={{1,0},{2,1},{3,2},{0,3},{5,4},{6,5},{7,6},{4,7},{9,8},{10,9},{11,1... | collective-permute-start | bytes 36872 | tf_op jit(solution)/shard_map/ppermute | solution.py:24
  86.7 3.2 %collective-permute-start.21 = (f32[6,1,512]{2,1,0:T(1,128)S(1)}, f32[6,1,512]{2,1,0:T(1,128)S(1)}, u32[]{:S(2)}, u32[]{:S(2)}) collective-permute-start(f32[6,1,512]{2,1,0:T(1,128)S(1)} %get-tuple-element.121), channel_id=1, source_target_pairs={{1,0},{2,1},{3,2},{0,3},{5,4},{6,5},{7,6},{4,7},{9,8},{10,9},{11,1... | collective-permute-start | bytes 36872 | tf_op jit(solution)/shard_map/ppermute | solution.py:24
  90.6 3.2 %collective-permute-start.23 = (f32[6,1,512]{2,1,0:T(1,128)S(1)}, f32[6,1,512]{2,1,0:T(1,128)S(1)}, u32[]{:S(2)}, u32[]{:S(2)}) collective-permute-start(f32[6,1,512]{2,1,0:T(1,128)S(1)} %get-tuple-element.119), channel_id=1, source_target_pairs={{1,0},{2,1},{3,2},{0,3},{5,4},{6,5},{7,6},{4,7},{9,8},{10,9},{11,1... | collective-permute-start | bytes 36872 | tf_op jit(solution)/shard_map/ppermute | solution.py:24
  94.5 3.2 %collective-permute-start.25 = (f32[6,1,512]{2,1,0:T(1,128)S(1)}, f32[6,1,512]{2,1,0:T(1,128)S(1)}, u32[]{:S(2)}, u32[]{:S(2)}) collective-permute-start(f32[6,1,512]{2,1,0:T(1,128)S(1)} %get-tuple-element.117), channel_id=1, source_target_pairs={{1,0},{2,1},{3,2},{0,3},{5,4},{6,5},{7,6},{4,7},{9,8},{10,9},{11,1... | collective-permute-start | bytes 36872 | tf_op jit(solution)/shard_map/ppermute | solution.py:24
  98.4 3.2 %collective-permute-start.27 = (f32[6,1,512]{2,1,0:T(1,128)S(1)}, f32[6,1,512]{2,1,0:T(1,128)S(1)}, u32[]{:S(2)}, u32[]{:S(2)}) collective-permute-start(f32[6,1,512]{2,1,0:T(1,128)S(1)} %get-tuple-element.115), channel_id=1, source_target_pairs={{1,0},{2,1},{3,2},{0,3},{5,4},{6,5},{7,6},{4,7},{9,8},{10,9},{11,1... | collective-permute-start | bytes 36872 | tf_op jit(solution)/shard_map/ppermute | solution.py:24
  102.3 3.3 %collective-permute-start.29 = (f32[6,1,512]{2,1,0:T(1,128)S(1)}, f32[6,1,512]{2,1,0:T(1,128)S(1)}, u32[]{:S(2)}, u32[]{:S(2)}) collective-permute-start(f32[6,1,512]{2,1,0:T(1,128)S(1)} %get-tuple-element.113), channel_id=1, source_target_pairs={{1,0},{2,1},{3,2},{0,3},{5,4},{6,5},{7,6},{4,7},{9,8},{10,9},{11,1... | collective-permute-start | bytes 36872 | tf_op jit(solution)/shard_map/ppermute | solution.py:24
  106.3 3.2 %collective-permute-start.31 = (f32[6,1,512]{2,1,0:T(1,128)S(1)}, f32[6,1,512]{2,1,0:T(1,128)S(1)}, u32[]{:S(2)}, u32[]{:S(2)}) collective-permute-start(f32[6,1,512]{2,1,0:T(1,128)S(1)} %get-tuple-element.111), channel_id=1, source_target_pairs={{1,0},{2,1},{3,2},{0,3},{5,4},{6,5},{7,6},{4,7},{9,8},{10,9},{11,1... | collective-permute-start | bytes 36872 | tf_op jit(solution)/shard_map/ppermute | solution.py:24
  110.1 8.7 %collective-permute-start.33 = (f32[6,16,512]{2,1,0:T(8,128)S(1)}, f32[6,16,512]{2,1,0:T(8,128)S(1)}, u32[]{:S(2)}, u32[]{:S(2)}) collective-permute-start(f32[6,16,512]{2,1,0:T(8,128)S(1)} %multiply_add_fusion.9), channel_id=1, source_target_pairs={{0,4},{4,8},{8,12},{12,16},{16,20},{20,24},{24,28},{1,5},{5,9},{9,... | collective-permute-start | bytes 589832 | tf_op jit(solution)/shard_map/ppermute | solution.py:34
  118.9 9.4 %collective-permute-start.34 = (f32[6,16,512]{2,1,0:T(8,128)S(1)}, f32[6,16,512]{2,1,0:T(8,128)S(1)}, u32[]{:S(2)}, u32[]{:S(2)}) collective-permute-start(f32[6,16,512]{2,1,0:T(8,128)S(1)} %subtract_select_fusion), channel_id=1, source_target_pairs={{0,4},{4,8},{8,12},{12,16},{16,20},{20,24},{24,28},{1,5},{5,9},{9,... | collective-permute-start | bytes 589832 | tf_op jit(solution)/shard_map/ppermute | solution.py:34
  129.7 3.1 %collective-permute-start.35 = (f32[6,1,512]{2,1,0:T(1,128)S(1)}, f32[6,1,512]{2,1,0:T(1,128)S(1)}, u32[]{:S(2)}, u32[]{:S(2)}) collective-permute-start(f32[6,1,512]{2,1,0:T(1,128)S(1)} %get-tuple-element.109), channel_id=1, source_target_pairs={{1,0},{2,1},{3,2},{0,3},{5,4},{6,5},{7,6},{4,7},{9,8},{10,9},{11,1... | collective-permute-start | bytes 36872 | tf_op jit(solution)/shard_map/ppermute | solution.py:24
  133.5 3.2 %collective-permute-start.37 = (f32[6,1,512]{2,1,0:T(1,128)S(1)}, f32[6,1,512]{2,1,0:T(1,128)S(1)}, u32[]{:S(2)}, u32[]{:S(2)}) collective-permute-start(f32[6,1,512]{2,1,0:T(1,128)S(1)} %get-tuple-element.107), channel_id=1, source_target_pairs={{1,0},{2,1},{3,2},{0,3},{5,4},{6,5},{7,6},{4,7},{9,8},{10,9},{11,1... | collective-permute-start | bytes 36872 | tf_op jit(solution)/shard_map/ppermute | solution.py:24
  137.4 3.2 %collective-permute-start.39 = (f32[6,1,512]{2,1,0:T(1,128)S(1)}, f32[6,1,512]{2,1,0:T(1,128)S(1)}, u32[]{:S(2)}, u32[]{:S(2)}) collective-permute-start(f32[6,1,512]{2,1,0:T(1,128)S(1)} %get-tuple-element.105), channel_id=1, source_target_pairs={{1,0},{2,1},{3,2},{0,3},{5,4},{6,5},{7,6},{4,7},{9,8},{10,9},{11,1... | collective-permute-start | bytes 36872 | tf_op jit(solution)/shard_map/ppermute | solution.py:24
  141.3 3.2 %collective-permute-start.41 = (f32[6,1,512]{2,1,0:T(1,128)S(1)}, f32[6,1,512]{2,1,0:T(1,128)S(1)}, u32[]{:S(2)}, u32[]{:S(2)}) collective-permute-start(f32[6,1,512]{2,1,0:T(1,128)S(1)} %get-tuple-element.103), channel_id=1, source_target_pairs={{1,0},{2,1},{3,2},{0,3},{5,4},{6,5},{7,6},{4,7},{9,8},{10,9},{11,1... | collective-permute-start | bytes 36872 | tf_op jit(solution)/shard_map/ppermute | solution.py:24
  145.1 9.5 %collective-permute-start.43 = (f32[6,16,512]{2,1,0:T(8,128)S(1)}, f32[6,16,512]{2,1,0:T(8,128)S(1)}, u32[]{:S(2)}, u32[]{:S(2)}) collective-permute-start(f32[6,16,512]{2,1,0:T(8,128)S(1)} %add_add_fusion.1), channel_id=1, source_target_pairs={{0,4},{4,8},{8,12},{12,16},{16,20},{20,24},{24,28},{1,5},{5,9},{9,... | collective-permute-start | bytes 589832 | tf_op jit(solution)/shard_map/ppermute | solution.py:34
  155.6 3.1 %collective-permute-start.44 = (f32[6,1,512]{2,1,0:T(1,128)S(1)}, f32[6,1,512]{2,1,0:T(1,128)S(1)}, u32[]{:S(2)}, u32[]{:S(2)}) collective-permute-start(f32[6,1,512]{2,1,0:T(1,128)S(1)} %get-tuple-element.101), channel_id=1, source_target_pairs={{1,0},{2,1},{3,2},{0,3},{5,4},{6,5},{7,6},{4,7},{9,8},{10,9},{11,1... | collective-permute-start | bytes 36872 | tf_op jit(solution)/shard_map/ppermute | solution.py:24
  159.4 3.2 %collective-permute-start.46 = (f32[6,1,512]{2,1,0:T(1,128)S(1)}, f32[6,1,512]{2,1,0:T(1,128)S(1)}, u32[]{:S(2)}, u32[]{:S(2)}) collective-permute-start(f32[6,1,512]{2,1,0:T(1,128)S(1)} %get-tuple-element.99), channel_id=1, source_target_pairs={{1,0},{2,1},{3,2},{0,3},{5,4},{6,5},{7,6},{4,7},{9,8},{10,9},{11,1... | collective-permute-start | bytes 36872 | tf_op jit(solution)/shard_map/ppermute | solution.py:24
  163.3 3.2 %collective-permute-start.48 = (f32[6,1,512]{2,1,0:T(1,128)S(1)}, f32[6,1,512]{2,1,0:T(1,128)S(1)}, u32[]{:S(2)}, u32[]{:S(2)}) collective-permute-start(f32[6,1,512]{2,1,0:T(1,128)S(1)} %get-tuple-element.97), channel_id=1, source_target_pairs={{1,0},{2,1},{3,2},{0,3},{5,4},{6,5},{7,6},{4,7},{9,8},{10,9},{11,1... | collective-permute-start | bytes 36872 | tf_op jit(solution)/shard_map/ppermute | solution.py:24
  167.2 3.2 %collective-permute-start.50 = (f32[6,1,512]{2,1,0:T(1,128)S(1)}, f32[6,1,512]{2,1,0:T(1,128)S(1)}, u32[]{:S(2)}, u32[]{:S(2)}) collective-permute-start(f32[6,1,512]{2,1,0:T(1,128)S(1)} %get-tuple-element.95), channel_id=1, source_target_pairs={{1,0},{2,1},{3,2},{0,3},{5,4},{6,5},{7,6},{4,7},{9,8},{10,9},{11,1... | collective-permute-start | bytes 36872 | tf_op jit(solution)/shard_map/ppermute | solution.py:24
  171.0 9.7 %collective-permute-start.52 = (f32[6,16,512]{2,1,0:T(8,128)S(1)}, f32[6,16,512]{2,1,0:T(8,128)S(1)}, u32[]{:S(2)}, u32[]{:S(2)}) collective-permute-start(f32[6,16,512]{2,1,0:T(8,128)S(1)} %add_add_fusion), channel_id=1, source_target_pairs={{0,4},{4,8},{8,12},{12,16},{16,20},{20,24},{24,28},{1,5},{5,9},{9,... | collective-permute-start | bytes 589832 | tf_op jit(solution)/shard_map/ppermute | solution.py:34
  185.2 3.2 %collective-permute-start.55 = (f32[6,1,512]{2,1,0:T(1,128)S(1)}, f32[6,1,512]{2,1,0:T(1,128)S(1)}, u32[]{:S(2)}, u32[]{:S(2)}) collective-permute-start(f32[6,1,512]{2,1,0:T(1,128)S(1)} %get-tuple-element.91), channel_id=1, source_target_pairs={{1,0},{2,1},{3,2},{0,3},{5,4},{6,5},{7,6},{4,7},{9,8},{10,9},{11,1... | collective-permute-start | bytes 36872 | tf_op jit(solution)/shard_map/ppermute | solution.py:24
  189.1 3.2 %collective-permute-start.57 = (f32[6,1,512]{2,1,0:T(1,128)S(1)}, f32[6,1,512]{2,1,0:T(1,128)S(1)}, u32[]{:S(2)}, u32[]{:S(2)}) collective-permute-start(f32[6,1,512]{2,1,0:T(1,128)S(1)} %get-tuple-element.89), channel_id=1, source_target_pairs={{1,0},{2,1},{3,2},{0,3},{5,4},{6,5},{7,6},{4,7},{9,8},{10,9},{11,1... | collective-permute-start | bytes 36872 | tf_op jit(solution)/shard_map/ppermute | solution.py:24
  193.0 3.2 %collective-permute-start.59 = (f32[6,1,512]{2,1,0:T(1,128)S(1)}, f32[6,1,512]{2,1,0:T(1,128)S(1)}, u32[]{:S(2)}, u32[]{:S(2)}) collective-permute-start(f32[6,1,512]{2,1,0:T(1,128)S(1)} %get-tuple-element.87), channel_id=1, source_target_pairs={{1,0},{2,1},{3,2},{0,3},{5,4},{6,5},{7,6},{4,7},{9,8},{10,9},{11,1... | collective-permute-start | bytes 36872 | tf_op jit(solution)/shard_map/ppermute | solution.py:24
  (36 other events, 136.0 us)
where the time goes:
time: 198 us; the launch traced here: 197 us
  waiting for transfers between devices  112 us (57%)
  other arithmetic  49.7 us (25%)
  starting transfers between devices  30.5 us (15%)
  local copies, waits for them, and re-layouts  2.96 us (1%)
  between operations  2.09 us (1%)
    ppermute x28, waiting for transfers between devices, padded_2(): lax.ppermute(head, axis, [((i + 1) % count, i) for i in range(count)])  57.8 us
    ppermute x5, waiting for transfers between devices, passed_along(): lax.ppermute(value, axis, [(source, source + steps) for source in range(i...  34.9 us
    unnamed x140, other arithmetic  24.9 us
    ppermute x28, waiting for transfers between devices, padded_2(): lax.ppermute(tail, axis, [(i, (i + 1) % count) for i in range(count)])  19.5 us
    ppermute x5, starting transfers between devices, passed_along(): lax.ppermute(value, axis, [(source, source + steps) for source in range(i...  11.2 us
    ppermute x28, starting transfers between devices, padded_2(): lax.ppermute(head, axis, [((i + 1) % count, i) for i in range(count)])  11 us
    ppermute x28, starting transfers between devices, padded_2(): lax.ppermute(tail, axis, [(i, (i + 1) % count) for i in range(count)])  8.19 us
    add x25, other arithmetic, advance(): return center + time_step * tendency  7.26 us
  transfers between devices with their start and end apart: 61, of which 61 were waited for; matrix products, arithmetic and copies ran while one was open for 0% of the time, Pallas kernels for 0%

commit v1 on v0

v1 whole, which is shorter than its diff:
```python
import functools

import jax
import jax.numpy as jnp
from jax import lax
from jax.experimental import pallas as pl
from jax.experimental.pallas import tpu as pltpu
from jax.sharding import PartitionSpec as P

STEPS_SLAB = 8
FINE = 0.1
NU = 0.5
SOUND_SQ = 1.0
COARSE = STEPS_SLAB * FINE / 4.0

MESH = pl.DeviceIdType.MESH
f32 = jnp.float32

ROWS = 16
TOP = 16
HEIGHT = 48
BLOCKS = 4
N_COEF = 10


def kernel(
    n_tm, n_space,
    cs, ini, bv, bs, bp, rr,
    corr, resid,
    F, K, X, HX, HB, HR, HY, PR, bst, brecv, ast, arecv, rst, cst, crecv, yst, est, erecv,
    ssem, rsem,
):
    tm = lax.axis_index("tm")
    sp = lax.axis_index("space")
    up = lax.rem(sp + n_space - 1, n_space)
    down = lax.rem(sp + 1, n_space)

    def cols(j):
        return pl.ds(128 * j, 128)

    barrier = pltpu.get_barrier_semaphore()
    pl.semaphore_signal(barrier, inc=1, device_id={"space": up}, device_id_type=MESH)
    pl.semaphore_signal(barrier, inc=1, device_id={"space": down}, device_id_type=MESH)
    for d in (1, 2, n_tm - 2, n_tm - 1):
        pl.semaphore_signal(barrier, inc=1, device_id={"tm": lax.rem(tm + d, n_tm)}, device_id_type=MESH)

    for c in range(6):
        X[c] = cs[0, c]
    X[6] = bv[...]
    X[7] = bs[...]
    X[8] = bp[0]
    X[9] = bp[1]
    X[10] = rr[...]
    zero8 = jnp.zeros((8, 128), f32)
    for b in range(2):
        for c in range(6):
            for j in range(BLOCKS):
                F[b, c, j, 0:8, :] = zero8
                F[b, c, j, 40:48, :] = zero8
    for b in range(2):
        for c in range(N_COEF):
            for j in range(BLOCKS):
                K[b, c, j, 0:8, :] = zero8
                K[b, c, j, 40:48, :] = zero8

    pl.semaphore_wait(barrier, 6)

    def halo(i, to_up, to_down, buf):
        a = pltpu.make_async_remote_copy(
            src_ref=to_up, dst_ref=buf.at[1], send_sem=ssem.at[2 * i], recv_sem=rsem.at[2 * i],
            device_id={"space": up}, device_id_type=MESH)
        b = pltpu.make_async_remote_copy(
            src_ref=to_down, dst_ref=buf.at[0], send_sem=ssem.at[2 * i + 1], recv_sem=rsem.at[2 * i + 1],
            device_id={"space": down}, device_id_type=MESH)
        a.start()
        b.start()
        return a, b

    def hop(i, src, dst, d):
        return pltpu.make_async_remote_copy(
            src_ref=src, dst_ref=dst, send_sem=ssem.at[8 + i], recv_sem=rsem.at[8 + i],
            device_id={"tm": lax.rem(tm + d, n_tm)}, device_id_type=MESH)

    def send(i, src, dst, d):
        @pl.when(tm + d < n_tm)
        def _():
            hop(i, src, dst, d).start()

    def sent(i, src, dst, d):
        @pl.when(tm + d < n_tm)
        def _():
            hop(i, src, dst, d).wait_send()

    def received(i, src, dst, d):
        @pl.when(tm >= d)
        def _():
            hop(i, src, dst, d).wait_recv()

    def set_coefs(rows, get):
        for j in range(BLOCKS):
            U, S, Pp, Q, R = [get(6 + i, j) for i in range(5)]
            for b, h in enumerate((FINE, COARSE)):
                k = 0.5 * h
                K[b, 0, j, rows, :] = k * U
                K[b, 1, j, rows, :] = h * S
                K[b, 2, j, rows, :] = (2.0 * h) * S
                K[b, 3, j, rows, :] = h * (Pp + R)
                K[b, 4, j, rows, :] = k * (Pp + R)
                K[b, 5, j, rows, :] = h * Q
                K[b, 6, j, rows, :] = k * Q
                K[b, 7, j, rows, :] = h * R
                K[b, 8, j, rows, :] = k * R
                K[b, 9, j, rows, :] = (1.0 - 4.0 * NU * h) - h * R

    def step(src, b, h, left):
        dst = 1 - src
        k = 0.5 * h
        c0 = 1.0 - 4.0 * NU * h
        c1 = NU * h
        lane = lax.broadcasted_iota(jnp.int32, (8, 128), 1)
        first = lane == 0
        last = lane == 127
        start = TOP - left
        tiles = (ROWS + 2 * left + 7) // 8

        def tile(t, carry):
            r = start + 8 * t
            here = pl.ds(r, 8)
            cen, rm, rp = {}, {}, {}

            def center(c, j):
                if (c, j) not in cen:
                    cen[c, j] = F[src, c, j, here, :]
                return cen[c, j]

            def minus(c, j):
                if j < 0:
                    return zero8
                if (c, j) not in rm:
                    rm[c, j] = pltpu.roll(center(c, j), 1, 1)
                return rm[c, j]

            def plus(c, j):
                if j >= BLOCKS:
                    return zero8
                if (c, j) not in rp:
                    rp[c, j] = pltpu.roll(center(c, j), 127, 1)
                return rp[c, j]

            for j in range(BLOCKS):
                f, dx, dy, sm = [], [], [], []
                for c in range(6):
                    xm = F[src, c, j, pl.ds(r - 1, 8), :]
                    xp = F[src, c, j, pl.ds(r + 1, 8), :]
                    ym = jnp.where(first, minus(c, j - 1), minus(c, j))
                    yp = jnp.where(last, plus(c, j + 1), plus(c, j))
                    f.append(center(c, j))
                    dx.append(xp - xm)
                    dy.append(yp - ym)
                    sm.append((xp + xm) + (yp + ym))
                kU, hS, h2S, hPR, kPR, hQ, kQ, hR, kR, d0 = [K[b, i, j, here, :] for i in range(N_COEF)]
                div = dx[0] + dy[1]
                out = [
                    c0 * f[0] + c1 * sm[0] + k * (dx[3] - dx[2] + dy[4]) - kU * dx[0] - hS * f[1],
                    c0 * f[1] + c1 * sm[1] + k * (dx[4] - dy[2] + dy[5]) - kU * dx[1],
                    c0 * f[2] + c1 * sm[2] - (k * SOUND_SQ) * div,
                    d0 * f[3] + c1 * sm[3] - kU * dx[3] + h2S * f[4] + hPR * dx[0] + hQ * dy[0],
                    d0 * f[4] + c1 * sm[4] - kU * dx[4] + hS * f[5] + kQ * div + kPR * dx[1] + kR * dy[0],
                    d0 * f[5] + c1 * sm[5] - kU * dx[5] + hQ * dx[1] + hR * dy[1],
                ]
                for c in range(6):
                    F[dst, c, j, here, :] = out[c]
            return carry

        lax.fori_loop(0, tiles, tile, 0)

    def steps(count, b, h):
        def pair(i, carry):
            step(0, b, h, count - 1 - 2 * i)
            step(1, b, h, count - 2 - 2 * i)
            return carry

        lax.fori_loop(0, count // 2, pair, 0)

    def put_halo(buf):
        for c in range(6):
            for j in range(BLOCKS):
                F[0, c, j, 8:16, :] = buf[0, c, j]
                F[0, c, j, 32:40, :] = buf[1, c, j]

    OWN = slice(TOP, TOP + ROWS)

    hx = halo(0, X.at[:, 0:8, :], X.at[:, 8:16, :], HX)
    for c in range(6):
        for j in range(BLOCKS):
            F[0, c, j, OWN, :] = X[c, :, cols(j)]
    set_coefs(OWN, lambda i, j: X[i, :, cols(j)])
    for a in hx:
        a.wait()
    for side, lo in ((0, 8), (1, 32)):
        rows = slice(lo, lo + 8)
        for c in range(6):
            for j in range(BLOCKS):
                F[0, c, j, rows, :] = HX[side, c, :, cols(j)]
        set_coefs(rows, lambda i, j: HX[side, i, :, cols(j)])
    steps(8, 0, FINE)

    for c in range(6):
        for j in range(BLOCKS):
            bst[c, j] = F[0, c, j, OWN, :]
    hb = halo(1, bst.at[:, :, 0:8, :], bst.at[:, :, 8:16, :], HB)
    send(0, bst, brecv, 1)
    for a in hb:
        a.wait()
    put_halo(HB)
    steps(8, 0, FINE)
    for c in range(6):
        for j in range(BLOCKS):
            ast[c, j] = F[0, c, j, OWN, :]
    send(1, ast, arecv, 2)

    received(0, bst, brecv, 1)
    received(1, ast, arecv, 2)

    @pl.when(tm == 0)
    def _():
        for c in range(6):
            for j in range(BLOCKS):
                brecv[c, j] = cs[0, c, :, cols(j)]
                rst[c, j] = ini[c, :, cols(j)] - cs[0, c, :, cols(j)]

    @pl.when(tm == 1)
    def _():
        for c in range(6):
            for j in range(BLOCKS):
                rst[c, j] = brecv[c, j] - brecv[c, j]

    @pl.when(tm >= 2)
    def _():
        for c in range(6):
            for j in range(BLOCKS):
                rst[c, j] = arecv[c, j] - brecv[c, j]

    for c in range(6):
        for j in range(BLOCKS):
            half = slice(4 * (j % 2), 4 * (j % 2) + 4)
            PR[0, c, j // 2, half, :] = rst[c, j, 0:4, :]
            PR[1, c, j // 2, half, :] = rst[c, j, 12:16, :]
    hr = halo(2, PR.at[0], PR.at[1], HR)
    for c in range(6):
        for j in range(BLOCKS):
            v = rst[c, j]
            resid[0, c, :, cols(j)] = v
            F[0, c, j, OWN, :] = v
    for a in hr:
        a.wait()
    for c in range(6):
        for j in range(BLOCKS):
            half = slice(4 * (j % 2), 4 * (j % 2) + 4)
            F[0, c, j, 12:16, :] = HR[0, c, j // 2, half, :]
            F[0, c, j, 32:36, :] = HR[1, c, j // 2, half, :]
    steps(4, 1, COARSE)
    for c in range(6):
        for j in range(BLOCKS):
            cst[c, j] = F[0, c, j, OWN, :]
    send(2, cst, crecv, 1)
    received(2, cst, crecv, 1)

    @pl.when(tm == 0)
    def _():
        yst[...] = rst[...]

    @pl.when(tm >= 1)
    def _():
        for c in range(6):
            for j in range(BLOCKS):
                yst[c, j] = rst[c, j] + crecv[c, j]

    hy = halo(3, yst.at[:, :, 0:8, :], yst.at[:, :, 8:16, :], HY)
    for c in range(6):
        for j in range(BLOCKS):
            F[0, c, j, OWN, :] = yst[c, j]
    for a in hy:
        a.wait()
    put_halo(HY)
    steps(8, 1, COARSE)
    for c in range(6):
        for j in range(BLOCKS):
            est[c, j] = F[0, c, j, OWN, :]
    send(3, est, erecv, 2)
    received(3, est, erecv, 2)

    @pl.when(tm < 2)
    def _():
        for c in range(6):
            for j in range(BLOCKS):
                corr[0, c, :, cols(j)] = brecv[c, j] + yst[c, j]

    @pl.when(tm >= 2)
    def _():
        for c in range(6):
            for j in range(BLOCKS):
                corr[0, c, :, cols(j)] = brecv[c, j] + (yst[c, j] + erecv[c, j])

    sent(0, bst, brecv, 1)
    sent(1, ast, arecv, 2)
    sent(2, cst, crecv, 1)
    sent(3, est, erecv, 2)


def per_device(n_tm, n_space, cs, ini, bv, bs, bp, rr):
    vmem = pl.BlockSpec(memory_space=pltpu.VMEM)
    strip = pltpu.VMEM((6, BLOCKS, ROWS, 128), f32)
    halo8 = pltpu.VMEM((2, 6, BLOCKS, 8, 128), f32)
    shape = jax.ShapeDtypeStruct(cs.shape, f32)
    return pl.pallas_call(
        functools.partial(kernel, n_tm, n_space),
        out_shape=(shape, shape),
        in_specs=[vmem] * 6,
        out_specs=(vmem, vmem),
        scratch_shapes=[
            pltpu.VMEM((2, 6, BLOCKS, HEIGHT, 128), f32),
            pltpu.VMEM((2, N_COEF, BLOCKS, HEIGHT, 128), f32),
            pltpu.VMEM((11, ROWS, 512), f32),
            pltpu.VMEM((2, 11, 8, 512), f32),
            halo8,
            pltpu.VMEM((2, 6, 2, 8, 128), f32),
            halo8,
            pltpu.VMEM((2, 6, 2, 8, 128), f32),
            strip, strip, strip, strip, strip, strip, strip, strip, strip, strip,
            pltpu.SemaphoreType.DMA((12,)),
            pltpu.SemaphoreType.DMA((12,)),
        ],
        compiler_params=pltpu.CompilerParams(
            collective_id=0, has_side_effects=True, vmem_limit_bytes=32 * 1024 * 1024
        ),
    )(cs, ini, bv, bs, bp, rr)


def solution(mesh):
    n_tm, n_space = mesh.shape["tm"], mesh.shape["space"]
    return jax.shard_map(
        functools.partial(per_device, n_tm, n_space),
        mesh=mesh,
        in_specs=(
            P("tm", None, "space", None),
            P(None, "space", None),
            P("space", None),
            P("space", None),
            P(None, "space", None),
            P("space", None),
        ),
        out_specs=(P("tm", None, "space", None), P("tm", None, "space", None)),
        check_vma=False,
    )
```

time: 198 us -> 57.3 us (0.29)
  waiting for transfers between devices: 112 us -> 0 us
  Pallas kernels: 0 us -> 49.8 us
  other arithmetic: 49.7 us -> 0 us
  starting transfers between devices: 30.5 us -> 0 us
  local copies, waits for them, and re-layouts: 2.96 us -> 6.31 us
    ppermute x61 -> x0, waiting for transfers between devices: 112 us -> none  [the longest x28 57.8 us: padded_2(): lax.ppermute(head, axis, [((i + 1) % count, i) for i in range(count)])]
    pallas_call x0 -> x1, Pallas kernels: none -> 49.8 us  [per_device(): pl.pallas_call(functools.partial(kernel, n_tm, n_space), out_shape=(shape...]
    ppermute x61 -> x0, starting transfers between devices: 30.5 us -> none  [the longest x5 11.2 us: passed_along(): lax.ppermute(value, axis, [(source, source + steps) for source in range(i...]
    unnamed x140 -> x0, other arithmetic: 24.9 us -> none
    add x27 -> x0, other arithmetic: 7.35 us -> none  [the longest x25 7.26 us: advance(): return center + time_step * tendency]
    concatenate x28 -> x0, other arithmetic: 7.19 us -> none  [padded_2(): jnp.concatenate([lax.ppermute(tail, axis, [(i, (i + 1) % count) for i in...]
    another operation x28 -> x0, other arithmetic: 5 us -> none  [advance(): tendency = jnp.stack([tend_u, tend_v, tend_p, tend_a, tend_b, tend_c], 0)]
    unnamed x14, local copies, waits for them, and re-layouts: 1.43 us -> 6.31 us
  transfers between devices with their start and end apart: 61 -> 0, of which waited for: 61 -> 0; matrix products, arithmetic and copies ran while one was open for 0% -> 0% of each run, Pallas kernels for 0% -> 0%
where the time goes in v1:
time: 57.3 us; the launch traced here: 56.7 us
  Pallas kernels  49.8 us (87%)
  local copies, waits for them, and re-layouts  6.31 us (11%)
  between operations  0.65 us (1%)
    pallas_call x1, Pallas kernels, per_device(): pl.pallas_call(functools.partial(kernel, n_tm, n_space), out_shape=(shape...  49.8 us
    unnamed x14, local copies, waits for them, and re-layouts  6.31 us

profile of v1, /device:TPU:25, one launch (start us, length us, event | category | flops | bytes accessed | tf_op | source)
XLA Modules:
  0.0 56.7 jit_solution(5658894726137475540)
XLA Ops:
  0.6 0.0 copy-start
  0.6 0.9 %copy-done = f32[1,6,16,512]{3,2,1,0:T(8,128)S(1)} copy-done((f32[1,6,16,512]{3,2,1,0:T(8,128)S(1)}, f32[1,6,16,512]{3,2,1,0:T(8,128)}, u32[]{:S(2)}) %copy-start) | copy-done | bytes 196632
  1.6 0.0 copy-start.1
  1.6 0.9 %copy-done.1 = f32[6,16,512]{2,1,0:T(8,128)S(1)} copy-done((f32[6,16,512]{2,1,0:T(8,128)S(1)}, f32[6,16,512]{2,1,0:T(8,128)}, u32[]{:S(2)}) %copy-start.1) | copy-done | bytes 196632
  2.5 0.0 copy-start.2
  2.5 0.8 %copy-done.2 = f32[2,16,512]{2,1,0:T(8,128)S(1)} copy-done((f32[2,16,512]{2,1,0:T(8,128)S(1)}, f32[2,16,512]{2,1,0:T(8,128)}, u32[]{:S(2)}) %copy-start.2) | copy-done | bytes 65560
  3.3 0.0 copy-start.3
  3.3 0.8 %copy-done.3 = f32[16,512]{1,0:T(8,128)S(1)} copy-done((f32[16,512]{1,0:T(8,128)S(1)}, f32[16,512]{1,0:T(8,128)}, u32[]{:S(2)}) %copy-start.3) | copy-done | bytes 32792
  4.1 0.0 copy-start.4
  4.1 0.8 %copy-done.4 = f32[16,512]{1,0:T(8,128)S(1)} copy-done((f32[16,512]{1,0:T(8,128)S(1)}, f32[16,512]{1,0:T(8,128)}, u32[]{:S(2)}) %copy-start.4) | copy-done | bytes 32792
  4.8 0.0 copy-start.5
  4.8 0.8 %copy-done.5 = f32[16,512]{1,0:T(8,128)S(1)} copy-done((f32[16,512]{1,0:T(8,128)S(1)}, f32[16,512]{1,0:T(8,128)}, u32[]{:S(2)}) %copy-start.5) | copy-done | bytes 32792
  5.6 49.8 %shard_map.77 = (f32[1,6,16,512]{3,2,1,0:T(8,128)S(1)}, f32[1,6,16,512]{3,2,1,0:T(8,128)S(1)}) custom-call(f32[1,6,16,512]{3,2,1,0:T(8,128)S(1)} %copy-done, f32[6,16,512]{2,1,0:T(8,128)S(1)} %copy-done.1, f32[16,512]{1,0:T(8,128)S(1)} %copy-done.3, f32[16,512]{1,0:T(8,128)S(1)} %copy-done.4, f32[2,16,512]{2,1,0:T(8,128)S(1)} %copy-done.2, ...), custom_call_target="tpu_custom_call" | custom-call | tf_op jit(solution)/shard_map/pallas_call | solution.py:316
  55.4 0.7 %copy.10 = f32[1,6,16,512]{3,2,1,0:T(8,128)} copy(f32[1,6,16,512]{3,2,1,0:T(8,128)S(1)} %get-tuple-element.4) | data formatting | bytes 393216
  56.1 0.7 %copy.11 = f32[1,6,16,512]{3,2,1,0:T(8,128)} copy(f32[1,6,16,512]{3,2,1,0:T(8,128)S(1)} %get-tuple-element.5) | data formatting | bytes 393216
Async XLA Ops:
  0.6 0.9 %copy-start = (f32[1,6,16,512]{3,2,1,0:T(8,128)S(1)}, f32[1,6,16,512]{3,2,1,0:T(8,128)}, u32[]{:S(2)}) copy-start(f32[1,6,16,512]{3,2,1,0:T(8,128)} %cs.1) | copy-start | bytes 589828
  1.6 0.9 %copy-start.1 = (f32[6,16,512]{2,1,0:T(8,128)S(1)}, f32[6,16,512]{2,1,0:T(8,128)}, u32[]{:S(2)}) copy-start(f32[6,16,512]{2,1,0:T(8,128)} %ini.1) | copy-start | bytes 589828
  2.5 0.8 %copy-start.2 = (f32[2,16,512]{2,1,0:T(8,128)S(1)}, f32[2,16,512]{2,1,0:T(8,128)}, u32[]{:S(2)}) copy-start(f32[2,16,512]{2,1,0:T(8,128)} %bp.1) | copy-start | bytes 196612
  3.3 0.8 %copy-start.3 = (f32[16,512]{1,0:T(8,128)S(1)}, f32[16,512]{1,0:T(8,128)}, u32[]{:S(2)}) copy-start(f32[16,512]{1,0:T(8,128)} %bv.1) | copy-start | bytes 98308
  4.1 0.8 %copy-start.4 = (f32[16,512]{1,0:T(8,128)S(1)}, f32[16,512]{1,0:T(8,128)}, u32[]{:S(2)}) copy-start(f32[16,512]{1,0:T(8,128)} %bs.1) | copy-start | bytes 98308
  4.8 0.8 %copy-start.5 = (f32[16,512]{1,0:T(8,128)S(1)}, f32[16,512]{1,0:T(8,128)}, u32[]{:S(2)}) copy-start(f32[16,512]{1,0:T(8,128)} %rr.1) | copy-start | bytes 98308

commit v2 on v1

--- a/solution.py
+++ b/solution.py
@@ -28,7 +28,7 @@
     cs, ini, bv, bs, bp, rr,
     corr, resid,
     F, K, X, HX, HB, HR, HY, PR, bst, brecv, ast, arecv, rst, cst, crecv, yst, est, erecv,
-    ssem, rsem,
+    start_field, ssem, rsem, lsem,
 ):
     tm = lax.axis_index("tm")
     sp = lax.axis_index("space")
@@ -41,16 +41,20 @@
     barrier = pltpu.get_barrier_semaphore()
     pl.semaphore_signal(barrier, inc=1, device_id={"space": up}, device_id_type=MESH)
     pl.semaphore_signal(barrier, inc=1, device_id={"space": down}, device_id_type=MESH)
-    for d in (1, 2, n_tm - 2, n_tm - 1):
-        pl.semaphore_signal(barrier, inc=1, device_id={"tm": lax.rem(tm + d, n_tm)}, device_id_type=MESH)
-
-    for c in range(6):
-        X[c] = cs[0, c]
-    X[6] = bv[...]
-    X[7] = bs[...]
-    X[8] = bp[0]
-    X[9] = bp[1]
-    X[10] = rr[...]
+    for d in (1, 2):
+        @pl.when(tm >= d)
+        def _():
+            pl.semaphore_signal(barrier, inc=1, device_id={"tm": tm - d}, device_id_type=MESH)
+
+    fetches = [
+        pltpu.make_async_copy(src, dst, lsem.at[i])
+        for i, (src, dst) in enumerate((
+            (cs.at[0], X.at[0:6]), (bv, X.at[6]), (bs, X.at[7]), (bp, X.at[8:10]), (rr, X.at[10]), (ini, start_field),
+        ))
+    ]
+    for a in fetches:
+        a.start()
+
     zero8 = jnp.zeros((8, 128), f32)
     for b in range(2):
         for c in range(6):
@@ -63,38 +67,41 @@
                 K[b, c, j, 0:8, :] = zero8
                 K[b, c, j, 40:48, :] = zero8
 
-    pl.semaphore_wait(barrier, 6)
-
-    def halo(i, to_up, to_down, buf):
+    for a in fetches:
+        a.wait()
+    pl.semaphore_wait(barrier, 4 - tm // (n_tm - 1) - tm // (n_tm - 2))
+
+    def exchange(i, to_up, to_down, from_up, from_down):
         a = pltpu.make_async_remote_copy(
-            src_ref=to_up, dst_ref=buf.at[1], send_sem=ssem.at[2 * i], recv_sem=rsem.at[2 * i],
+            src_ref=to_up, dst_ref=from_down, send_sem=ssem.at[i], recv_sem=rsem.at[i],
             device_id={"space": up}, device_id_type=MESH)
         b = pltpu.make_async_remote_copy(
-            src_ref=to_down, dst_ref=buf.at[0], send_sem=ssem.at[2 * i + 1], recv_sem=rsem.at[2 * i + 1],
+            src_ref=to_down, dst_ref=from_up, send_sem=ssem.at[i + 1], recv_sem=rsem.at[i + 1],
             device_id={"space": down}, device_id_type=MESH)
         a.start()
         b.start()
-        return a, b
-
-    def hop(i, src, dst, d):
+        return [a, b]
+
+    def hop(i, src, dst, d, j):
         return pltpu.make_async_remote_copy(
-            src_ref=src, dst_ref=dst, send_sem=ssem.at[8 + i], recv_sem=rsem.at[8 + i],
+            src_ref=src.at[:, j], dst_ref=dst.at[:, j], send_sem=ssem.at[i + j], recv_sem=rsem.at[i + j],
             device_id={"tm": lax.rem(tm + d, n_tm)}, device_id_type=MESH)
 
-    def send(i, src, dst, d):
+    def send(i, src, dst, d, j):
         @pl.when(tm + d < n_tm)
         def _():
-            hop(i, src, dst, d).start()
+            hop(i, src, dst, d, j).start()
 
     def sent(i, src, dst, d):
         @pl.when(tm + d < n_tm)
         def _():
-            hop(i, src, dst, d).wait_send()
-
-    def received(i, src, dst, d):
+            for j in range(BLOCKS):
+                hop(i, src, dst, d, j).wait_send()
+
+    def received(i, src, dst, d, j):
         @pl.when(tm >= d)
         def _():
-            hop(i, src, dst, d).wait_recv()
+            hop(i, src, dst, d, j).wait_recv()
 
     def set_coefs(rows, get):
         for j in range(BLOCKS):
@@ -112,7 +119,7 @@
                 K[b, 8, j, rows, :] = k * R
                 K[b, 9, j, rows, :] = (1.0 - 4.0 * NU * h) - h * R
 
-    def step(src, b, h, left):
+    def step(src, b, h, left, tiles):
         dst = 1 - src
         k = 0.5 * h
         c0 = 1.0 - 4.0 * NU * h
@@ -121,9 +128,8 @@
         first = lane == 0
         last = lane == 127
         start = TOP - left
-        tiles = (ROWS + 2 * left + 7) // 8
-
-        def tile(t, carry):
+
+        def tile(t):
             r = start + 8 * t
             here = pl.ds(r, 8)
             cen, rm, rp = {}, {}, {}
@@ -170,17 +176,22 @@
                 ]
                 for c in range(6):
                     F[dst, c, j, here, :] = out[c]
-            return carry
-
-        lax.fori_loop(0, tiles, tile, 0)
+
+        for t in range(tiles):
+            tile(t)
 
     def steps(count, b, h):
-        def pair(i, carry):
-            step(0, b, h, count - 1 - 2 * i)
-            step(1, b, h, count - 2 - 2 * i)
-            return carry
-
-        lax.fori_loop(0, count // 2, pair, 0)
+        def pairs(first, end, tiles):
+            def pair(i, carry):
+                step(0, b, h, count - 1 - 2 * i, tiles)
+                step(1, b, h, count - 2 - 2 * i, tiles)
+                return carry
+
+            lax.fori_loop(first, end, pair, 0)
+
+        if count > 4:
+            pairs(0, (count - 4) // 2, 4)
+        pairs((count - 4) // 2, count // 2, 3)
 
     def put_halo(buf):
         for c in range(6):
@@ -190,9 +201,12 @@
 
     OWN = slice(TOP, TOP + ROWS)
 
-    hx = halo(0, X.at[:, 0:8, :], X.at[:, 8:16, :], HX)
-    for c in range(6):
-        for j in range(BLOCKS):
+    BLK = range(BLOCKS)
+    S_X, S_B, S_R, S_Y, S_H = 0, 2, 4, 8, 16
+
+    hx = exchange(S_X, X.at[:, 0:8, :], X.at[:, 8:16, :], HX.at[0], HX.at[1])
+    for c in range(6):
+        for j in BLK:
             F[0, c, j, OWN, :] = X[c, :, cols(j)]
     set_coefs(OWN, lambda i, j: X[i, :, cols(j)])
     for a in hx:
@@ -200,112 +214,116 @@
     for side, lo in ((0, 8), (1, 32)):
         rows = slice(lo, lo + 8)
         for c in range(6):
-            for j in range(BLOCKS):
+            for j in BLK:
                 F[0, c, j, rows, :] = HX[side, c, :, cols(j)]
         set_coefs(rows, lambda i, j: HX[side, i, :, cols(j)])
     steps(8, 0, FINE)
 
     for c in range(6):
-        for j in range(BLOCKS):
+        for j in BLK:
             bst[c, j] = F[0, c, j, OWN, :]
-    hb = halo(1, bst.at[:, :, 0:8, :], bst.at[:, :, 8:16, :], HB)
-    send(0, bst, brecv, 1)
+    hb = exchange(S_B, bst.at[:, :, 0:8, :], bst.at[:, :, 8:16, :], HB.at[0], HB.at[1])
+    for j in BLK:
+        send(S_H, bst, brecv, 1, j)
     for a in hb:
         a.wait()
     put_halo(HB)
     steps(8, 0, FINE)
-    for c in range(6):
-        for j in range(BLOCKS):
+    for j in BLK:
+        for c in range(6):
             ast[c, j] = F[0, c, j, OWN, :]
-    send(1, ast, arecv, 2)
-
-    received(0, bst, brecv, 1)
-    received(1, ast, arecv, 2)
-
-    @pl.when(tm == 0)
-    def _():
-        for c in range(6):
-            for j in range(BLOCKS):
-                brecv[c, j] = cs[0, c, :, cols(j)]
-                rst[c, j] = ini[c, :, cols(j)] - cs[0, c, :, cols(j)]
-
-    @pl.when(tm == 1)
-    def _():
-        for c in range(6):
-            for j in range(BLOCKS):
+        send(S_H + 4, ast, arecv, 2, j)
+
+    hr = []
+    for j in BLK:
+        received(S_H, bst, brecv, 1, j)
+        received(S_H + 4, ast, arecv, 2, j)
+
+        @pl.when(tm == 0)
+        def _():
+            for c in range(6):
+                brecv[c, j] = X[c, :, cols(j)]
+                rst[c, j] = start_field[c, :, cols(j)] - X[c, :, cols(j)]
+
+        @pl.when(tm == 1)
+        def _():
+            for c in range(6):
                 rst[c, j] = brecv[c, j] - brecv[c, j]
 
-    @pl.when(tm >= 2)
-    def _():
-        for c in range(6):
-            for j in range(BLOCKS):
+        @pl.when(tm >= 2)
+        def _():
+            for c in range(6):
                 rst[c, j] = arecv[c, j] - brecv[c, j]
 
-    for c in range(6):
-        for j in range(BLOCKS):
-            half = slice(4 * (j % 2), 4 * (j % 2) + 4)
+        half = slice(4 * (j % 2), 4 * (j % 2) + 4)
+        for c in range(6):
             PR[0, c, j // 2, half, :] = rst[c, j, 0:4, :]
             PR[1, c, j // 2, half, :] = rst[c, j, 12:16, :]
-    hr = halo(2, PR.at[0], PR.at[1], HR)
-    for c in range(6):
-        for j in range(BLOCKS):
+        if j % 2:
+            p = j // 2
+            hr += exchange(S_R + 2 * p, PR.at[0, :, p], PR.at[1, :, p], HR.at[0, :, p], HR.at[1, :, p])
+    for c in range(6):
+        for j in BLK:
             v = rst[c, j]
             resid[0, c, :, cols(j)] = v
             F[0, c, j, OWN, :] = v
     for a in hr:
         a.wait()
     for c in range(6):
-        for j in range(BLOCKS):
+        for j in BLK:
             half = slice(4 * (j % 2), 4 * (j % 2) + 4)
             F[0, c, j, 12:16, :] = HR[0, c, j // 2, half, :]
             F[0, c, j, 32:36, :] = HR[1, c, j // 2, half, :]
     steps(4, 1, COARSE)
-    for c in range(6):
-        for j in range(BLOCKS):
+    for j in BLK:
+        for c in range(6):
             cst[c, j] = F[0, c, j, OWN, :]
-    send(2, cst, crecv, 1)
-    received(2, cst, crecv, 1)
-
-    @pl.when(tm == 0)
-    def _():
-        yst[...] = rst[...]
-
-    @pl.when(tm >= 1)
-    def _():
-        for c in range(6):
-            for j in range(BLOCKS):
+        send(S_H + 8, cst, crecv, 1, j)
+
+    hy = []
+    for j in BLK:
+        received(S_H + 8, cst, crecv, 1, j)
+
+        @pl.when(tm == 0)
+        def _():
+            for c in range(6):
+                yst[c, j] = rst[c, j]
+
+        @pl.when(tm >= 1)
+        def _():
+            for c in range(6):
                 yst[c, j] = rst[c, j] + crecv[c, j]
 
-    hy = halo(3, yst.at[:, :, 0:8, :], yst.at[:, :, 8:16, :], HY)
-    for c in range(6):
-        for j in range(BLOCKS):
+        hy += exchange(S_Y + 2 * j, yst.at[:, j, 0:8, :], yst.at[:, j, 8:16, :], HY.at[0, :, j], HY.at[1, :, j])
+    for c in range(6):
+        for j in BLK:
             F[0, c, j, OWN, :] = yst[c, j]
     for a in hy:
         a.wait()
     put_halo(HY)
     steps(8, 1, COARSE)
-    for c in range(6):
-        for j in range(BLOCKS):
+    for j in BLK:
+        for c in range(6):
             est[c, j] = F[0, c, j, OWN, :]
-    send(3, est, erecv, 2)
-    received(3, est, erecv, 2)
-
-    @pl.when(tm < 2)
-    def _():
-        for c in range(6):
-            for j in range(BLOCKS):
+        send(S_H + 12, est, erecv, 2, j)
+
+    for j in BLK:
+        received(S_H + 12, est, erecv, 2, j)
+
+        @pl.when(tm < 2)
+        def _():
+            for c in range(6):
                 corr[0, c, :, cols(j)] = brecv[c, j] + yst[c, j]
 
-    @pl.when(tm >= 2)
-    def _():
-        for c in range(6):
-            for j in range(BLOCKS):
+        @pl.when(tm >= 2)
+        def _():
+            for c in range(6):
                 corr[0, c, :, cols(j)] = brecv[c, j] + (yst[c, j] + erecv[c, j])
 
-    sent(0, bst, brecv, 1)
-    sent(1, ast, arecv, 2)
-    sent(2, cst, crecv, 1)
-    sent(3, est, erecv, 2)
+    sent(S_H, bst, brecv, 1)
+    sent(S_H + 4, ast, arecv, 2)
+    sent(S_H + 8, cst, crecv, 1)
+    sent(S_H + 12, est, erecv, 2)
 
 
 def per_device(n_tm, n_space, cs, ini, bv, bs, bp, rr):
@@ -316,7 +334,7 @@
     return pl.pallas_call(
         functools.partial(kernel, n_tm, n_space),
         out_shape=(shape, shape),
-        in_specs=[vmem] * 6,
+        in_specs=[pl.BlockSpec(memory_space=pl.ANY)] * 6,
         out_specs=(vmem, vmem),
         scratch_shapes=[
             pltpu.VMEM((2, 6, BLOCKS, HEIGHT, 128), f32),
@@ -328,11 +346,13 @@
             halo8,
             pltpu.VMEM((2, 6, 2, 8, 128), f32),
             strip, strip, strip, strip, strip, strip, strip, strip, strip, strip,
-            pltpu.SemaphoreType.DMA((12,)),
-            pltpu.SemaphoreType.DMA((12,)),
+            pltpu.VMEM((6, ROWS, 512), f32),
+            pltpu.SemaphoreType.DMA((32,)),
+            pltpu.SemaphoreType.DMA((32,)),
+            pltpu.SemaphoreType.DMA((6,)),
         ],
         compiler_params=pltpu.CompilerParams(
-            collective_id=0, has_side_effects=True, vmem_limit_bytes=32 * 1024 * 1024
+            collective_id=0, has_side_effects=True, vmem_limit_bytes=60 * 1024 * 1024
         ),
     )(cs, ini, bv, bs, bp, rr)
 

time: 57.3 us -> 45.7 us (0.80)
  Pallas kernels: 49.8 us -> 42.6 us
  local copies, waits for them, and re-layouts: 6.31 us -> 2.34 us
    pallas_call x1, Pallas kernels: 49.8 us -> 42.6 us  [per_device(): pl.pallas_call(functools.partial(kernel, n_tm, n_space), out_shape=(shape...]
    unnamed x14 -> x4, local copies, waits for them, and re-layouts: 6.31 us -> 2.34 us
where the time goes in v2:
time: 45.7 us; the launch traced here: 45.6 us
  Pallas kernels  42.6 us (93%)
  local copies, waits for them, and re-layouts  2.34 us (5%)
  between operations  0.65 us (1%)
    pallas_call x1, Pallas kernels, per_device(): pl.pallas_call(functools.partial(kernel, n_tm, n_space), out_shape=(shape...  42.6 us
    unnamed x4, local copies, waits for them, and re-layouts  2.34 us

profile of v2, /device:TPU:25, one launch (start us, length us, event | category | flops | bytes accessed | tf_op | source)
XLA Modules:
  0.0 45.6 jit_solution(7756962715594952957)
XLA Ops:
  0.6 42.6 %shard_map.77 = (f32[1,6,16,512]{3,2,1,0:T(8,128)}, f32[1,6,16,512]{3,2,1,0:T(8,128)}) custom-call(f32[1,6,16,512]{3,2,1,0:T(8,128)} %cs.1, f32[6,16,512]{2,1,0:T(8,128)} %ini.1, f32[16,512]{1,0:T(8,128)} %bv.1, f32[16,512]{1,0:T(8,128)} %bs.1, f32[2,16,512]{2,1,0:T(8,128)} %bp.1, f32[16,512]{1,0:T(8,128)} %rr.1), custom_call_target="tpu_custom_call" | custom-call | tf_op jit(solution)/shard_map/pallas_call | solution.py:334
  43.2 0.0 copy-start
  43.2 1.7 %copy.10 = f32[1,6,16,512]{3,2,1,0:T(8,128)} copy(f32[1,6,16,512]{3,2,1,0:T(8,128)} %get-tuple-element.4) | data formatting | bytes 393216
  44.9 0.0 copy-done
  44.9 0.7 %copy.11 = f32[1,6,16,512]{3,2,1,0:T(8,128)} copy(f32[1,6,16,512]{3,2,1,0:T(8,128)S(1)} %copy-done) | data formatting | bytes 393216
Async XLA Ops:
  43.2 1.7 %copy-start = (f32[1,6,16,512]{3,2,1,0:T(8,128)S(1)}, f32[1,6,16,512]{3,2,1,0:T(8,128)}, u32[]{:S(2)}) copy-start(f32[1,6,16,512]{3,2,1,0:T(8,128)} %get-tuple-element.5) | copy-start | bytes 589828

commit v3 on v2

--- a/solution.py
+++ b/solution.py
@@ -28,7 +28,7 @@
     cs, ini, bv, bs, bp, rr,
     corr, resid,
     F, K, X, HX, HB, HR, HY, PR, bst, brecv, ast, arecv, rst, cst, crecv, yst, est, erecv,
-    start_field, ssem, rsem, lsem,
+    start_field, rbuf, cbuf, ssem, rsem, lsem,
 ):
     tm = lax.axis_index("tm")
     sp = lax.axis_index("space")
@@ -202,27 +202,33 @@
     OWN = slice(TOP, TOP + ROWS)
 
     BLK = range(BLOCKS)
-    S_X, S_B, S_R, S_Y, S_H = 0, 2, 4, 8, 16
-
-    hx = exchange(S_X, X.at[:, 0:8, :], X.at[:, 8:16, :], HX.at[0], HX.at[1])
+    S_X, S_B, S_R, S_Y, S_H = 0, 8, 16, 20, 28
+
+    hx = []
+    for i, part in enumerate((slice(6, 9), slice(9, 11), slice(0, 3), slice(3, 6))):
+        hx += exchange(S_X + 2 * i, X.at[part, 0:8, :], X.at[part, 8:16, :], HX.at[0, part], HX.at[1, part])
     for c in range(6):
         for j in BLK:
             F[0, c, j, OWN, :] = X[c, :, cols(j)]
     set_coefs(OWN, lambda i, j: X[i, :, cols(j)])
-    for a in hx:
-        a.wait()
-    for side, lo in ((0, 8), (1, 32)):
-        rows = slice(lo, lo + 8)
+    halves = ((0, slice(8, 16)), (1, slice(32, 40)))
+    for a in hx[:4]:
+        a.wait()
+    for side, rows in halves:
+        set_coefs(rows, lambda i, j: HX[side, i, :, cols(j)])
+    for a in hx[4:]:
+        a.wait()
+    for side, rows in halves:
         for c in range(6):
             for j in BLK:
                 F[0, c, j, rows, :] = HX[side, c, :, cols(j)]
-        set_coefs(rows, lambda i, j: HX[side, i, :, cols(j)])
     steps(8, 0, FINE)
 
-    for c in range(6):
-        for j in BLK:
+    hb = []
+    for j in BLK:
+        for c in range(6):
             bst[c, j] = F[0, c, j, OWN, :]
-    hb = exchange(S_B, bst.at[:, :, 0:8, :], bst.at[:, :, 8:16, :], HB.at[0], HB.at[1])
+        hb += exchange(S_B + 2 * j, bst.at[:, j, 0:8, :], bst.at[:, j, 8:16, :], HB.at[0, :, j], HB.at[1, :, j])
     for j in BLK:
         send(S_H, bst, brecv, 1, j)
     for a in hb:
@@ -265,8 +271,10 @@
     for c in range(6):
         for j in BLK:
             v = rst[c, j]
-            resid[0, c, :, cols(j)] = v
+            rbuf[c, :, cols(j)] = v
             F[0, c, j, OWN, :] = v
+    outs = [pltpu.make_async_copy(rbuf, resid.at[0], lsem.at[6])]
+    outs[0].start()
     for a in hr:
         a.wait()
     for c in range(6):
@@ -313,13 +321,19 @@
         @pl.when(tm < 2)
         def _():
             for c in range(6):
-                corr[0, c, :, cols(j)] = brecv[c, j] + yst[c, j]
+                cbuf[c, :, cols(j)] = brecv[c, j] + yst[c, j]
 
         @pl.when(tm >= 2)
         def _():
             for c in range(6):
-                corr[0, c, :, cols(j)] = brecv[c, j] + (yst[c, j] + erecv[c, j])
-
+                cbuf[c, :, cols(j)] = brecv[c, j] + (yst[c, j] + erecv[c, j])
+
+        out = pltpu.make_async_copy(cbuf.at[:, :, cols(j)], corr.at[0, :, :, cols(j)], lsem.at[7 + j])
+        out.start()
+        outs.append(out)
+
+    for a in outs:
+        a.wait()
     sent(S_H, bst, brecv, 1)
     sent(S_H + 4, ast, arecv, 2)
     sent(S_H + 8, cst, crecv, 1)
@@ -327,7 +341,6 @@
 
 
 def per_device(n_tm, n_space, cs, ini, bv, bs, bp, rr):
-    vmem = pl.BlockSpec(memory_space=pltpu.VMEM)
     strip = pltpu.VMEM((6, BLOCKS, ROWS, 128), f32)
     halo8 = pltpu.VMEM((2, 6, BLOCKS, 8, 128), f32)
     shape = jax.ShapeDtypeStruct(cs.shape, f32)
@@ -335,7 +348,7 @@
         functools.partial(kernel, n_tm, n_space),
         out_shape=(shape, shape),
         in_specs=[pl.BlockSpec(memory_space=pl.ANY)] * 6,
-        out_specs=(vmem, vmem),
+        out_specs=(pl.BlockSpec(memory_space=pl.ANY),) * 2,
         scratch_shapes=[
             pltpu.VMEM((2, 6, BLOCKS, HEIGHT, 128), f32),
             pltpu.VMEM((2, N_COEF, BLOCKS, HEIGHT, 128), f32),
@@ -346,10 +359,10 @@
             halo8,
             pltpu.VMEM((2, 6, 2, 8, 128), f32),
             strip, strip, strip, strip, strip, strip, strip, strip, strip, strip,
-            pltpu.VMEM((6, ROWS, 512), f32),
-            pltpu.SemaphoreType.DMA((32,)),
-            pltpu.SemaphoreType.DMA((32,)),
-            pltpu.SemaphoreType.DMA((6,)),
+            pltpu.VMEM((6, ROWS, 512), f32), pltpu.VMEM((6, ROWS, 512), f32), pltpu.VMEM((6, ROWS, 512), f32),
+            pltpu.SemaphoreType.DMA((44,)),
+            pltpu.SemaphoreType.DMA((44,)),
+            pltpu.SemaphoreType.DMA((11,)),
         ],
         compiler_params=pltpu.CompilerParams(
             collective_id=0, has_side_effects=True, vmem_limit_bytes=60 * 1024 * 1024

time: 45.7 us -> 45.8 us (level)
  no operation moved by 1% of the time
where the time goes in v3:
time: 45.8 us; the launch traced here: 45.6 us
  Pallas kernels  42.6 us (93%)
  local copies, waits for them, and re-layouts  2.34 us (5%)
  between operations  0.65 us (1%)
    pallas_call x1, Pallas kernels, per_device(): pl.pallas_call(functools.partial(kernel, n_tm, n_space), out_shape=(shape...  42.6 us
    unnamed x4, local copies, waits for them, and re-layouts  2.34 us

profile of v3, /device:TPU:25, one launch (start us, length us, event | category | flops | bytes accessed | tf_op | source)
XLA Modules:
  0.0 45.6 jit_solution(8635162644405457537)
XLA Ops:
  0.6 42.6 %shard_map.77 = (f32[1,6,16,512]{3,2,1,0:T(8,128)}, f32[1,6,16,512]{3,2,1,0:T(8,128)}) custom-call(f32[1,6,16,512]{3,2,1,0:T(8,128)} %cs.1, f32[6,16,512]{2,1,0:T(8,128)} %ini.1, f32[16,512]{1,0:T(8,128)} %bv.1, f32[16,512]{1,0:T(8,128)} %bs.1, f32[2,16,512]{2,1,0:T(8,128)} %bp.1, f32[16,512]{1,0:T(8,128)} %rr.1), custom_call_target="tpu_custom_call" | custom-call | tf_op jit(solution)/shard_map/pallas_call | solution.py:347
  43.3 0.0 copy-start
  43.3 1.7 %copy.10 = f32[1,6,16,512]{3,2,1,0:T(8,128)} copy(f32[1,6,16,512]{3,2,1,0:T(8,128)} %get-tuple-element.4) | data formatting | bytes 393216
  44.9 0.0 copy-done
  44.9 0.7 %copy.11 = f32[1,6,16,512]{3,2,1,0:T(8,128)} copy(f32[1,6,16,512]{3,2,1,0:T(8,128)S(1)} %copy-done) | data formatting | bytes 393216
Async XLA Ops:
  43.3 1.7 %copy-start = (f32[1,6,16,512]{3,2,1,0:T(8,128)S(1)}, f32[1,6,16,512]{3,2,1,0:T(8,128)}, u32[]{:S(2)}) copy-start(f32[1,6,16,512]{3,2,1,0:T(8,128)} %get-tuple-element.5) | copy-start | bytes 589828
